TPU v7x, 32 devices: a whole 2x2x4 slice. The times are simulated.
32 devices in a mesh: group: 2 (over x), wx: 16 (over z, y, core).
Axes of the slice: x: 2, y: 2, z: 4, core: 2. Of those that a mesh axis runs over, the one named last changes fastest.
Arguments:
- hidden_in: bfloat16 [8, 16384], P('group', 'wx'), parts along dimension 0, may hold values from -4000 to 4000
- norm_gain: bfloat16 [16384], P('wx'), may hold values from 0.099609375 to 1.8984375
- w_query: bfloat16 [16384, 8192], P('wx'), may hold values from -0.0625 to 0.0625
- w_key: bfloat16 [16384, 512], P('wx'), may hold values from -0.0625 to 0.0625
- w_value: bfloat16 [16384, 512], P('wx'), may hold values from -0.0625 to 0.0625
- w_out: bfloat16 [8192, 16384], P('wx'), may hold values from -0.1875 to 0.1875
- key_cache: bfloat16 [32, 8192, 128], P(('group', 'wx')), parts along dimension 0, may hold values from -800 to 800
- value_cache: bfloat16 [32, 8192, 128], P(('group', 'wx')), parts along dimension 0, may hold values from -6 to 6
- lengths: int32 [8], P('group'), parts along dimension 0, may hold values from 16 to 8192, as said below
Outputs:
- block_out: bfloat16 [8, 16384], P('group', 'wx'), parts along dimension 0
There are 2 independent parts, one for each index of `group`. A program takes and returns all parts, laid end to end along the dimension named above; an argument that names none is the same for every part. Nothing has to cross between parts.
Inputs may be any that keep to these rules, and one draw needn't show every extreme that they name: `lengths`: some row holds exactly 8192 cached tokens and some row exactly 16.
All inputs are finite; a program needn't handle non-finite values.
Results may differ from a plain program's by a relative error of at most 0.012.
The roundings to bfloat16 on the way count: a program that leaves them out, or rounds other values in their place, can miss the bound.
Values may be sent and summed in bfloat16 or wider, within the bound.
A program may use at most 128 MiB of HBM per device.

v0:
```python
import jax
import jax.numpy as jnp
from jax import lax
from jax.sharding import PartitionSpec as P

D = 16384
HD = 128
KVH = 4
G = 16


def attend_slot(query_heads, key_block, value_block, fresh_key, fresh_value, length):
    factor = HD ** (-0.5)
    scores = jnp.dot(query_heads, key_block.T, preferred_element_type=jnp.float32) * factor
    positions = jnp.arange(key_block.shape[0], dtype=jnp.int32)
    scores = jnp.where(positions[None, :] < length, scores, -jnp.inf)
    own_score = jnp.dot(query_heads, fresh_key, preferred_element_type=jnp.float32) * factor
    highest = jnp.maximum(jnp.max(scores, axis=1), own_score)
    weights = jnp.exp(scores - highest[:, None])
    own_weight = jnp.exp(own_score - highest)
    total = jnp.sum(weights, axis=1) + own_weight
    probs = weights.astype(jnp.bfloat16)
    own_prob = own_weight.astype(jnp.bfloat16)
    summed = jnp.dot(probs, value_block, preferred_element_type=jnp.float32)
    summed = (
        summed + own_prob.astype(jnp.float32)[:, None] * fresh_value.astype(jnp.float32)[None, :]
    )
    return (summed / total[:, None]).astype(jnp.bfloat16)


def local(hidden_in, norm_gain, w_query, w_key, w_value, w_out, key_cache, value_cache, lengths):
    batch = hidden_in.shape[0]
    slots_here = key_cache.shape[0]
    first_slot = lax.axis_index("wx") * slots_here
    widened = hidden_in.astype(jnp.float32)
    squares = lax.psum(jnp.sum(widened * widened, axis=1), "wx")
    inverse = lax.rsqrt(squares / D + 1e-05)
    slot_inverse = jnp.repeat(inverse, KVH)
    scaled = (widened * norm_gain.astype(jnp.float32)[None, :]).astype(jnp.bfloat16)
    query_part = jnp.dot(scaled, w_query, preferred_element_type=jnp.float32).reshape(
        batch, KVH, G * HD
    )
    key_part = jnp.dot(scaled, w_key, preferred_element_type=jnp.float32).reshape(batch, KVH, HD)
    value_part = jnp.dot(scaled, w_value, preferred_element_type=jnp.float32).reshape(
        batch, KVH, HD
    )
    terms = jnp.concatenate([query_part, key_part, value_part], axis=2).reshape(
        batch * KVH, (G + 2) * HD
    )
    scaled_terms = terms * slot_inverse[:, None]
    reduced = lax.psum_scatter(scaled_terms, "wx", scatter_dimension=0, tiled=True)
    query = reduced[:, : G * HD].astype(jnp.bfloat16).reshape(slots_here, G, HD)
    new_key = reduced[:, G * HD : (G + 1) * HD].astype(jnp.bfloat16)
    new_value = reduced[:, (G + 1) * HD :].astype(jnp.bfloat16)
    row_ids = (first_slot + jnp.arange(slots_here, dtype=jnp.int32)) // KVH
    slot_lengths = jnp.take(lengths, row_ids)
    attended = jax.vmap(attend_slot)(
        query, key_cache, value_cache, new_key, new_value, slot_lengths
    )
    gathered = lax.all_gather(attended.reshape(slots_here, G * HD), "wx", axis=0, tiled=True)
    flat = gathered.reshape(batch, KVH * G * HD)
    rows_here = w_out.shape[0]
    mine = lax.dynamic_slice_in_dim(flat, lax.axis_index("wx") * rows_here, rows_here, 1)
    partial_out = jnp.dot(mine, w_out, preferred_element_type=jnp.float32)
    block_out = lax.psum_scatter(partial_out, "wx", scatter_dimension=1, tiled=True).astype(
        jnp.bfloat16
    )
    return block_out


def solution(mesh):
    in_specs = (
        P("group", "wx"),
        P("wx"),
        P("wx", None),
        P("wx", None),
        P("wx", None),
        P("wx", None),
        P(("group", "wx"), None, None),
        P(("group", "wx"), None, None),
        P("group"),
    )
    out_specs = P("group", "wx")
    return jax.shard_map(local, mesh=mesh, in_specs=in_specs, out_specs=out_specs, check_vma=False)
```

profile of v0, /device:TPU:0, one launch (start us, length us, event | category | flops | bytes accessed | tf_op | source)
XLA Modules:
  0.0 265.5 jit_solution(5255596137160033286)
XLA Ops:
  6.5 0.0 copy-start
  6.5 0.0 reduce-scatter.4.cloned.1.call-start
  6.5 1.0 fusion.19
  7.5 34.9 %psum.7 = f32[4]{0:T(128)S(1)} all-reduce(f32[4]{0:T(128)S(1)} %fusion.19), channel_id=1, replica_groups=mesh['group'=2,'wx'=16] {'wx'}, use_global_device_ids=true, to_apply=%region_1.0 | all-reduce | flops 4 | bytes 32 | tf_op jit(solution)/shard_map/psum | solution.py:36
  42.4 0.1 broadcast_in_dim.28
  42.5 0.1 mul.56
  42.6 0.7 convert_element_type.33
  43.3 1.5 fusion.27
  44.8 1.5 fusion.25
  46.3 0.0 copy-start.2
  46.3 0.0 copy-start.1
  46.3 8.1 %fusion.29 = f32[4,8192]{1,0:T(4,128)S(1)} fusion(bf16[1024,8192]{1,0:T(8,128)(2,1)} %param.11, bf16[4,1024]{1,0:T(4,128)(2,1)} %param.9, f32[1024]{0:T(1024)S(1)} %convert_element_type.33), kind=kOutput, calls=%fused_computation.35 | convolution fusion | flops 67121152 | bytes 16920576 | tf_op jit(solution)/shard_map/dot_general | solution.py:40
  54.4 0.1 concatenate.10
  54.5 0.1 maximum_multiply_fusion
  54.6 59.2 %all-reduce.2 = bf16[16,2304]{1,0:T(8,128)(2,1)S(1)} all-reduce(f32[16,2304]{1,0:T(8,128)S(1)} %maximum_multiply_fusion), channel_id=2, replica_groups=mesh['group'=2,'wx'=16] {'wx'}, use_global_device_ids=true, to_apply=%region_2.0.clone | all-reduce | flops 36864 | bytes 221184
  113.7 0.0 copy-done.2
  113.7 0.6 dynamic-slice.3
  114.3 0.7 dynamic-slice_convert_fusion
  115.0 0.0 copy-done.1
  115.1 0.6 dynamic-slice.2
  116.3 0.0 copy-done
  116.3 0.8 fusion.32
  117.1 0.1 convert_convert_fusion
  117.2 0.3 fusion.14
  117.5 2.1 fusion.10
  119.6 17.7 %all-gather = bf16[16,1,2048]{2,1,0:T(2,128)(2,1)S(1)} all-gather(bf16[1,1,2048]{2,1,0:T(2,128)(2,1)S(1)} %reshape.127), channel_id=1, replica_groups=mesh['group'=2,'wx'=16] {'wx'}, dimensions={0}, use_global_device_ids=true | all-gather | bytes 69632 | tf_op jit(solution)/shard_map/all_gather | solution.py:60
  137.3 0.4 reduce.5
  137.6 0.1 reshape.98
  137.7 15.6 %convolution_bitcast_fusion = f32[16384,4]{1,0:T(8,128)} fusion(bf16[512,16384]{1,0:T(8,128)(2,1)} %param.14, bf16[4,8192]{1,0:T(4,128)(2,1)S(1)} %reshape.98, s32[]{:T(128)S(6)} %select_n.25), kind=kOutput, calls=%fused_computation | convolution fusion | flops 67108864 | bytes 17043460
  153.3 0.0 reduce-scatter.4.cloned.1.call-update
  153.3 103.5 %reduce-scatter.4.cloned.1.call-done = f32[1024,4]{1,0:T(8,128)} async-done(((f32[16384,4]{1,0:T(8,128)}), f32[1024,4]{1,0:T(8,128)}) %reduce-scatter.4.cloned.1.call-update) | async-done | bytes 16400
  256.8 1.8 copy.12
  (8 shorter events, 0.1 us)
Async XLA Ops:
  6.5 109.8 %copy-start = (bf16[1,8192,128]{2,1,0:T(8,128)(2,1)S(1)}, bf16[1,8192,128]{2,1,0:T(8,128)(2,1)}, u32[]{:S(2)}) copy-start(bf16[1,8192,128]{2,1,0:T(8,128)(2,1)} %param.15) | copy-start | bytes 6291460
  6.5 250.3 %reduce-scatter.4.cloned.1.call-start = ((), (), s32[]{:S(2)}) async-start(), calls=%async_computation.1 | async-start | bytes 8912896
  46.3 67.4 %copy-start.2 = (u32[32]{0:T(128)S(1)}, u32[32]{0:T(128)}, u32[]{:S(2)}) copy-start(u32[32]{0:T(128)} %constant.84) | copy-start | bytes 388
  46.3 68.8 %copy-start.1 = (s32[4]{0:T(128)S(1)}, s32[4]{0:T(128)}, u32[]{:S(2)}) copy-start(s32[4]{0:T(128)} %param.17) | copy-start | bytes 52
Sparse Core Ops, SparseCore 0:
  153.5 103.2 reduce-scatter.3
where the time goes:
time: 266 us; the launch traced here: 265 us
  blocking collectives  112 us (42%)
  waiting for transfers between devices  103 us (39%)
  matrix products  29.6 us (11%)
  between operations  14.2 us (5%)
  local copies, waits for them, and re-layouts  4.07 us (2%)
    unnamed x2, waiting for transfers between devices  103 us
    unnamed x1, blocking collectives  59.2 us
    psum x1, blocking collectives, local(): squares = lax.psum(jnp.sum(widened * widened, axis=1), 'wx')  34.9 us
    all_gather x1, blocking collectives, local(): lax.all_gather(attended.reshape(slots_here, G * HD), 'wx', axis=0, tiled=...  17.7 us
    unnamed x1, matrix products  15.6 us
    dot_general x1, matrix products, local(): jnp.dot(scaled, w_query, preferred_element_type=jnp.float32)  8.09 us
  transfers between devices with their start and end apart: 1, of which 1 were waited for; matrix products, arithmetic and copies ran while one was open for 0% of the time, Pallas kernels for 0%

commit v1 on v0

--- a/solution.py
+++ b/solution.py
@@ -1,6 +1,10 @@
+import functools
+
 import jax
 import jax.numpy as jnp
 from jax import lax
+from jax.experimental import pallas as pl
+from jax.experimental.pallas import tpu as pltpu
 from jax.sharding import PartitionSpec as P
 
 D = 16384
@@ -68,6 +72,318 @@
     return block_out
 
 
+MSG = 24
+QCOLS = 1024
+SCORE_BLOCK = 2048
+
+
+def fused_kernel(
+    n, batch, hidden_ref, gain_ref, lengths_ref, wq_hbm, wk_hbm, wv_hbm, wo_hbm, kc_hbm, vc_hbm,
+    out_ref, wq, wkv, wo, kc, vc, terms, terms_in, scores, att_out, att_in, parts_out, parts_in,
+    own_part, wq_sem, wkv_sem, wo_sem, cache_sem, a_send, a_recv, c_send, c_recv, d_send, d_recv,
+):
+    me = lax.axis_index("wx")
+    my_row = me // KVH
+    my_head = me % KVH
+    halves = G * HD // QCOLS
+    q_chunks = KVH * halves
+    kv_cols = KVH * HD
+    ctx = kc.shape[0]
+    out_cols = wo.shape[1] // n
+    blocks = out_cols // HD
+    wo_rows = wo.shape[0]
+    wo_piece = wo_rows // 4
+    heads_here = wo_rows // HD
+
+    def head_at(step):
+        return (my_head + 1 + step) % KVH
+
+    def key_weight_copy():
+        return pltpu.make_async_copy(wk_hbm, wkv.at[:, pl.ds(0, kv_cols)], wkv_sem.at[0])
+
+    def value_weight_copy():
+        return pltpu.make_async_copy(wv_hbm, wkv.at[:, pl.ds(kv_cols, kv_cols)], wkv_sem.at[1])
+
+    def query_weight_copy(step, half):
+        start = pl.multiple_of(head_at(step) * (G * HD) + half * QCOLS, QCOLS)
+        chunk = step * halves + half
+        return pltpu.make_async_copy(
+            wq_hbm.at[:, pl.ds(start, QCOLS)], wq.at[chunk], wq_sem.at[chunk]
+        )
+
+    def cache_copy(which):
+        source, target = ((kc_hbm, kc), (vc_hbm, vc))[which]
+        return pltpu.make_async_copy(source.at[0], target, cache_sem.at[which])
+
+    def out_weight_copy(piece):
+        rows = pl.ds(piece * wo_piece, wo_piece)
+        return pltpu.make_async_copy(wo_hbm.at[rows], wo.at[rows], wo_sem.at[piece])
+
+    key_weight_copy().start()
+    value_weight_copy().start()
+    for chunk in range(q_chunks):
+        query_weight_copy(chunk // halves, chunk % halves).start()
+
+    barrier = pltpu.get_barrier_semaphore()
+
+    def greet(k, carry):
+        pl.semaphore_signal(
+            barrier, inc=1, device_id={"wx": (me + k) % n}, device_id_type=pl.DeviceIdType.MESH
+        )
+        return carry
+
+    lax.fori_loop(1, n, greet, 0)
+
+    widened = hidden_ref[...].astype(jnp.float32)
+    scaled = (widened * gain_ref[...].astype(jnp.float32)).astype(jnp.bfloat16)
+    squares = jnp.broadcast_to(jnp.sum(widened * widened, axis=1, keepdims=True), (batch, HD))
+    terms[...] = jnp.zeros_like(terms)
+    for head in range(KVH):
+        terms[pl.ds(head * MSG + G + 2, batch, stride=KVH * MSG), :] = squares
+
+    key_weight_copy().wait()
+    value_weight_copy().wait()
+    fresh = jnp.dot(scaled, wkv[...], preferred_element_type=jnp.float32)
+    for head in range(KVH):
+        for which in range(2):
+            column = which * kv_cols + head * HD
+            terms[pl.ds(head * MSG + G + which, batch, stride=KVH * MSG), :] = fresh[
+                :, column : column + HD
+            ]
+
+    pl.semaphore_wait(barrier, n - 1)
+
+    def terms_copy(target):
+        place = (me - target + n) % n - 1
+        return pltpu.make_async_remote_copy(
+            src_ref=terms.at[pl.ds(pl.multiple_of(target * MSG, MSG), MSG)],
+            dst_ref=terms_in.at[place],
+            send_sem=a_send,
+            recv_sem=a_recv,
+            device_id={"wx": target},
+            device_id_type=pl.DeviceIdType.MESH,
+        )
+
+    for step in range(KVH):
+        head = head_at(step)
+        for half in range(halves):
+            query_weight_copy(step, half).wait()
+            chunk = step * halves + half
+            if chunk == q_chunks - 4:
+                cache_copy(0).start()
+            if chunk == q_chunks - 3:
+                cache_copy(1).start()
+            if chunk >= q_chunks - 2:
+                first = 2 * (chunk - q_chunks + 2)
+                out_weight_copy(first).start()
+                out_weight_copy(first + 1).start()
+            part = jnp.dot(scaled, wq[chunk], preferred_element_type=jnp.float32)
+            for j in range(QCOLS // HD):
+                row = head * MSG + half * (QCOLS // HD) + j
+                terms[pl.ds(row, batch, stride=KVH * MSG), :] = part[:, j * HD : (j + 1) * HD]
+        for row in range(batch):
+            target = row * KVH + head
+
+            @pl.when(target != me)
+            def _():
+                terms_copy(target).start()
+
+    def all_terms():
+        return pltpu.make_async_remote_copy(
+            src_ref=terms_in,
+            dst_ref=terms_in,
+            send_sem=a_send,
+            recv_sem=a_recv,
+            device_id={"wx": (me + 1) % n},
+            device_id_type=pl.DeviceIdType.MESH,
+        )
+
+    cache_copy(0).wait()
+    all_terms().wait_recv()
+    total_terms = terms[pl.ds(pl.multiple_of(me * MSG, MSG), MSG), :]
+    for k in range(n - 1):
+        total_terms = total_terms + terms_in[k]
+    inverse = lax.rsqrt(total_terms[G + 2 : G + 3] / D + 1e-05)
+    rounded = (total_terms[: G + 2] * inverse).astype(jnp.bfloat16)
+    query = rounded[:G]
+    new_key = rounded[G : G + 1].astype(jnp.float32)
+    new_value = rounded[G + 1 : G + 2].astype(jnp.float32)
+
+    factor = HD ** (-0.5)
+    length = lengths_ref[my_row]
+    own_score = jnp.sum(query.astype(jnp.float32) * new_key, axis=1, keepdims=True) * factor
+    highest = own_score
+    for c in range(ctx // SCORE_BLOCK):
+        span = pl.ds(c * SCORE_BLOCK, SCORE_BLOCK)
+        piece = lax.dot_general(
+            query, kc[span, :], (((1,), (1,)), ((), ())), preferred_element_type=jnp.float32
+        ) * factor
+        positions = lax.broadcasted_iota(jnp.int32, piece.shape, 1) + c * SCORE_BLOCK
+        piece = jnp.where(positions < length, piece, -jnp.inf)
+        scores[:, span] = piece
+        highest = jnp.maximum(highest, jnp.max(piece, axis=1, keepdims=True))
+    own_weight = jnp.exp(own_score - highest)
+    total = own_weight
+    summed = own_weight.astype(jnp.bfloat16).astype(jnp.float32) * new_value
+    cache_copy(1).wait()
+    for c in range(ctx // SCORE_BLOCK):
+        span = pl.ds(c * SCORE_BLOCK, SCORE_BLOCK)
+        weights = jnp.exp(scores[:, span] - highest)
+        total = total + jnp.sum(weights, axis=1, keepdims=True)
+        summed = summed + jnp.dot(
+            weights.astype(jnp.bfloat16), vc[span, :], preferred_element_type=jnp.float32
+        )
+    attended = (summed / total).astype(jnp.bfloat16).astype(jnp.float32)
+
+    sharers = G // heads_here
+    for i in range(sharers):
+        att_out[i, :heads_here] = attended[i * heads_here : (i + 1) * heads_here]
+
+    def attended_copy(i, row, target):
+        return pltpu.make_async_remote_copy(
+            src_ref=att_out.at[i],
+            dst_ref=att_in.at[row],
+            send_sem=c_send.at[i],
+            recv_sem=c_recv.at[row],
+            device_id={"wx": target},
+            device_id_type=pl.DeviceIdType.MESH,
+        )
+
+    for i in range(sharers):
+        target = my_head * sharers + i
+
+        @pl.when(target != me)
+        def _():
+            attended_copy(i, my_row, target).start()
+
+        @pl.when(target == me)
+        def _():
+            att_in[my_row] = att_out[i]
+
+    for piece in range(4):
+        out_weight_copy(piece).wait()
+    for row in range(batch):
+        source = row * KVH + me // sharers
+
+        @pl.when(source != me)
+        def _():
+            attended_copy(0, row, source).wait_recv()
+
+    everything = att_in[...]
+    mine = jnp.concatenate([everything[:, j] for j in range(heads_here)], axis=1).astype(
+        jnp.bfloat16
+    )
+
+    def product(target):
+        start = pl.multiple_of(target * out_cols, out_cols)
+        part = jnp.dot(mine, wo[:, pl.ds(start, out_cols)], preferred_element_type=jnp.float32)
+        return jnp.concatenate([part[:, b * HD : (b + 1) * HD] for b in range(blocks)], axis=0)
+
+    def send_part(i, carry):
+        k = n // 2 + (1 - 2 * (i % 2)) * ((i + 1) // 2)
+        target = (me + k) % n
+        parts_out[k - 1] = product(target).astype(jnp.bfloat16)
+        pltpu.make_async_remote_copy(
+            src_ref=parts_out.at[k - 1],
+            dst_ref=parts_in.at[k - 1],
+            send_sem=d_send,
+            recv_sem=d_recv,
+            device_id={"wx": target},
+            device_id_type=pl.DeviceIdType.MESH,
+        ).start()
+        return carry
+
+    lax.fori_loop(0, n - 1, send_part, 0)
+    result = product(me)
+    all_parts = pltpu.make_async_remote_copy(
+        src_ref=parts_out,
+        dst_ref=parts_in,
+        send_sem=d_send,
+        recv_sem=d_recv,
+        device_id={"wx": (me + 1) % n},
+        device_id_type=pl.DeviceIdType.MESH,
+    )
+    all_parts.wait_recv()
+    for k in range(n - 1):
+        result = result + parts_in[k].astype(jnp.float32)
+    out_ref[...] = jnp.concatenate(
+        [result[b * batch : (b + 1) * batch] for b in range(blocks)], axis=1
+    ).astype(jnp.bfloat16)
+
+    all_parts.wait_send()
+    all_terms().wait_send()
+    for i in range(sharers):
+        target = my_head * sharers + i
+
+        @pl.when(target != me)
+        def _():
+            attended_copy(i, my_row, target).wait_send()
+
+
+def fused(n, hidden_in, norm_gain, w_query, w_key, w_value, w_out, key_cache, value_cache, lengths):
+    batch, features = hidden_in.shape
+    ctx = key_cache.shape[1]
+    out_cols = w_out.shape[1] // n
+    part_rows = batch * out_cols // HD
+    q_chunks = w_query.shape[1] // QCOLS
+    vmem = pl.BlockSpec(memory_space=pltpu.VMEM)
+    hbm = pl.BlockSpec(memory_space=pl.ANY)
+    smem = pl.BlockSpec(memory_space=pltpu.SMEM)
+    bf16, f32 = jnp.bfloat16, jnp.float32
+    return pl.pallas_call(
+        functools.partial(fused_kernel, n, batch),
+        out_shape=jax.ShapeDtypeStruct((batch, out_cols), bf16),
+        in_specs=[vmem, vmem, smem] + [hbm] * 6,
+        out_specs=vmem,
+        scratch_shapes=[
+            pltpu.VMEM((q_chunks, features, QCOLS), bf16),
+            pltpu.VMEM((features, 2 * KVH * HD), bf16),
+            pltpu.VMEM(w_out.shape, bf16),
+            pltpu.VMEM((ctx, HD), bf16),
+            pltpu.VMEM((ctx, HD), bf16),
+            pltpu.VMEM((n * MSG, HD), f32),
+            pltpu.VMEM((n - 1, MSG, HD), f32),
+            pltpu.VMEM((G, ctx), f32),
+            pltpu.VMEM((G * HD // w_out.shape[0], 8, HD), f32),
+            pltpu.VMEM((batch, 8, HD), f32),
+            pltpu.VMEM((n - 1, part_rows, HD), bf16),
+            pltpu.VMEM((n - 1, part_rows, HD), bf16),
+            pltpu.VMEM((part_rows, HD), f32),
+            pltpu.SemaphoreType.DMA((q_chunks,)),
+            pltpu.SemaphoreType.DMA((2,)),
+            pltpu.SemaphoreType.DMA((4,)),
+            pltpu.SemaphoreType.DMA((2,)),
+            pltpu.SemaphoreType.DMA,
+            pltpu.SemaphoreType.DMA,
+            pltpu.SemaphoreType.DMA((G * HD // w_out.shape[0],)),
+            pltpu.SemaphoreType.DMA((batch,)),
+            pltpu.SemaphoreType.DMA,
+            pltpu.SemaphoreType.DMA,
+        ],
+        compiler_params=pltpu.CompilerParams(
+            collective_id=0, has_side_effects=True, vmem_limit_bytes=56 * 1024 * 1024
+        ),
+    )(
+        hidden_in, norm_gain.reshape(1, features), lengths, w_query, w_key, w_value, w_out,
+        key_cache, value_cache,
+    )
+
+
+def choose(n, *arrays):
+    hidden_in, w_out, key_cache = arrays[0], arrays[5], arrays[6]
+    rows_here = w_out.shape[0]
+    fits = (
+        key_cache.shape[0] == 1
+        and hidden_in.shape[0] * KVH == n
+        and rows_here % HD == 0
+        and (G * HD) % rows_here == 0
+        and rows_here <= 8 * HD
+        and key_cache.shape[1] % SCORE_BLOCK == 0
+        and (hidden_in.shape[0] * (w_out.shape[1] // n // HD)) % 16 == 0
+    )
+    return fused(n, *arrays) if fits else local(*arrays)
+
+
 def solution(mesh):
     in_specs = (
         P("group", "wx"),
@@ -81,4 +397,5 @@
         P("group"),
     )
     out_specs = P("group", "wx")
-    return jax.shard_map(local, mesh=mesh, in_specs=in_specs, out_specs=out_specs, check_vma=False)
+    return jax.shard_map(
+        functools.partial(choose, mesh.shape["wx"]), mesh=mesh, in_specs=in_specs, out_specs=out_specs, check_vma=False)

time: 266 us -> 31.8 us (0.12)
  blocking collectives: 112 us -> 0 us
  waiting for transfers between devices: 103 us -> 0 us
  matrix products: 29.6 us -> 0 us
  Pallas kernels: 0 us -> 28.9 us
  between operations: 14.2 us -> 0.01 us
    unnamed x2 -> x0, waiting for transfers between devices: 103 us -> none
    unnamed x1 -> x0, blocking collectives: 59.2 us -> none
    psum x1 -> x0, blocking collectives: 34.9 us -> none  [local(): squares = lax.psum(jnp.sum(widened * widened, axis=1), 'wx')]
    pallas_call x0 -> x1, Pallas kernels: none -> 28.9 us  [fused(): pl.pallas_call(functools.partial(fused_kernel, n, batch), out_shape=jax.S...]
    all_gather x1 -> x0, blocking collectives: 17.7 us -> none  [local(): lax.all_gather(attended.reshape(slots_here, G * HD), 'wx', axis=0, tiled=...]
    unnamed x1 -> x0, matrix products: 15.6 us -> none
    dot_general x6 -> x0, matrix products: 14 us -> none  [the longest x1 8.09 us: local(): jnp.dot(scaled, w_query, preferred_element_type=jnp.float32)]
  transfers between devices with their start and end apart: 1 -> 0, of which waited for: 1 -> 0; matrix products, arithmetic and copies ran while one was open for 0% -> 0% of each run, Pallas kernels for 0% -> 0%
where the time goes in v1:
time: 31.8 us; the launch traced here: 31.5 us
  Pallas kernels  28.9 us (91%)
  local copies, waits for them, and re-layouts  2.58 us (8%)
    pallas_call x1, Pallas kernels, fused(): pl.pallas_call(functools.partial(fused_kernel, n, batch), out_shape=jax.S...  28.9 us
    unnamed x1, local copies, waits for them, and re-layouts  1.3 us
    reshape x1, local copies, waits for them, and re-layouts, fused(): norm_gain.reshape(1, features)  1.28 us

profile of v1, /device:TPU:0, one launch (start us, length us, event | category | flops | bytes accessed | tf_op | source)
XLA Modules:
  0.0 31.5 jit_solution(4456513783873545781)
XLA Ops:
  0.0 1.3 %reshape.3.gain_ref = bf16[1,1024]{1,0:T(2,128)(2,1)} reshape(bf16[1024]{0:T(1024)(128)(2,1)} %param.10) | data formatting | bytes 4096 | tf_op jit(solution)/shard_map/reshape | solution.py:367
  1.3 28.9 %shard_map.91 = bf16[4,1024]{1,0:T(4,128)(2,1)} custom-call(bf16[4,1024]{1,0:T(4,128)(2,1)} %hidden_ref.1, bf16[1,1024]{1,0:T(2,128)(2,1)} %reshape.3.gain_ref, s32[4]{0:T(128)} %lengths_ref.1, bf16[1024,8192]{1,0:T(8,128)(2,1)} %wq_hbm.1, bf16[1024,512]{1,0:T(8,128)(2,1)} %wk_hbm.1, bf16[1024,512]{1,0:T(8,128)(2,1)} %wv_hbm.1, bf16[512,16384]{1,0:T(8,128)(2,1)} %wo_hbm.1, ...), custom_call_target="tpu_custom_call" | custom-call | tf_op jit(solution)/shard_map/pallas_call | solution.py:333
  30.2 1.3 %copy.11 = bf16[4,1024]{1,0:T(4,128)(2,1)} copy(bf16[4,1024]{1,0:T(4,128)(2,1)} %shard_map.91) | data formatting | bytes 16384

commit v2 on v1

--- a/solution.py
+++ b/solution.py
@@ -75,12 +75,14 @@
 MSG = 24
 QCOLS = 1024
 SCORE_BLOCK = 2048
+IN_FLIGHT = 4
+WO_PIECES = 8
 
 
 def fused_kernel(
     n, batch, hidden_ref, gain_ref, lengths_ref, wq_hbm, wk_hbm, wv_hbm, wo_hbm, kc_hbm, vc_hbm,
     out_ref, wq, wkv, wo, kc, vc, terms, terms_in, scores, att_out, att_in, parts_out, parts_in,
-    own_part, wq_sem, wkv_sem, wo_sem, cache_sem, a_send, a_recv, c_send, c_recv, d_send, d_recv,
+    wq_sem, wkv_sem, wo_sem, cache_sem, a_send, a_recv, c_send, c_recv, d_send, d_recv,
 ):
     me = lax.axis_index("wx")
     my_row = me // KVH
@@ -92,7 +94,8 @@
     out_cols = wo.shape[1] // n
     blocks = out_cols // HD
     wo_rows = wo.shape[0]
-    wo_piece = wo_rows // 4
+    wo_pieces = wo_sem.shape[0]
+    wo_piece = wo_rows // wo_pieces
     heads_here = wo_rows // HD
 
     def head_at(step):
@@ -119,10 +122,20 @@
         rows = pl.ds(piece * wo_piece, wo_piece)
         return pltpu.make_async_copy(wo_hbm.at[rows], wo.at[rows], wo_sem.at[piece])
 
-    key_weight_copy().start()
-    value_weight_copy().start()
-    for chunk in range(q_chunks):
-        query_weight_copy(chunk // halves, chunk % halves).start()
+    stream = [key_weight_copy, value_weight_copy]
+    stream += [
+        functools.partial(query_weight_copy, chunk // halves, chunk % halves)
+        for chunk in range(q_chunks)
+    ]
+    stream += [functools.partial(cache_copy, which) for which in range(2)]
+    stream += [functools.partial(out_weight_copy, piece) for piece in range(wo_pieces)]
+
+    def start_next(count):
+        for _ in range(count):
+            if stream:
+                stream.pop(0)().start()
+
+    start_next(2 + IN_FLIGHT)
 
     barrier = pltpu.get_barrier_semaphore()
 
@@ -135,7 +148,7 @@
     lax.fori_loop(1, n, greet, 0)
 
     widened = hidden_ref[...].astype(jnp.float32)
-    scaled = (widened * gain_ref[...].astype(jnp.float32)).astype(jnp.bfloat16)
+    scaled = (widened * gain_ref[...].astype(jnp.float32).reshape(1, -1)).astype(jnp.bfloat16)
     squares = jnp.broadcast_to(jnp.sum(widened * widened, axis=1, keepdims=True), (batch, HD))
     terms[...] = jnp.zeros_like(terms)
     for head in range(KVH):
@@ -169,14 +182,7 @@
         for half in range(halves):
             query_weight_copy(step, half).wait()
             chunk = step * halves + half
-            if chunk == q_chunks - 4:
-                cache_copy(0).start()
-            if chunk == q_chunks - 3:
-                cache_copy(1).start()
-            if chunk >= q_chunks - 2:
-                first = 2 * (chunk - q_chunks + 2)
-                out_weight_copy(first).start()
-                out_weight_copy(first + 1).start()
+            start_next(1)
             part = jnp.dot(scaled, wq[chunk], preferred_element_type=jnp.float32)
             for j in range(QCOLS // HD):
                 row = head * MSG + half * (QCOLS // HD) + j
@@ -198,7 +204,10 @@
             device_id_type=pl.DeviceIdType.MESH,
         )
 
-    cache_copy(0).wait()
+    for which in range(2):
+        cache_copy(which).wait()
+        start_next(2)
+    start_next(wo_pieces)
     all_terms().wait_recv()
     total_terms = terms[pl.ds(pl.multiple_of(me * MSG, MSG), MSG), :]
     for k in range(n - 1):
@@ -225,7 +234,6 @@
     own_weight = jnp.exp(own_score - highest)
     total = own_weight
     summed = own_weight.astype(jnp.bfloat16).astype(jnp.float32) * new_value
-    cache_copy(1).wait()
     for c in range(ctx // SCORE_BLOCK):
         span = pl.ds(c * SCORE_BLOCK, SCORE_BLOCK)
         weights = jnp.exp(scores[:, span] - highest)
@@ -260,7 +268,7 @@
         def _():
             att_in[my_row] = att_out[i]
 
-    for piece in range(4):
+    for piece in range(wo_pieces):
         out_weight_copy(piece).wait()
     for row in range(batch):
         source = row * KVH + me // sharers
@@ -348,10 +356,9 @@
             pltpu.VMEM((batch, 8, HD), f32),
             pltpu.VMEM((n - 1, part_rows, HD), bf16),
             pltpu.VMEM((n - 1, part_rows, HD), bf16),
-            pltpu.VMEM((part_rows, HD), f32),
             pltpu.SemaphoreType.DMA((q_chunks,)),
             pltpu.SemaphoreType.DMA((2,)),
-            pltpu.SemaphoreType.DMA((4,)),
+            pltpu.SemaphoreType.DMA((WO_PIECES,)),
             pltpu.SemaphoreType.DMA((2,)),
             pltpu.SemaphoreType.DMA,
             pltpu.SemaphoreType.DMA,
@@ -364,7 +371,7 @@
             collective_id=0, has_side_effects=True, vmem_limit_bytes=56 * 1024 * 1024
         ),
     )(
-        hidden_in, norm_gain.reshape(1, features), lengths, w_query, w_key, w_value, w_out,
+        hidden_in, norm_gain, lengths, w_query, w_key, w_value, w_out,
         key_cache, value_cache,
     )
 
@@ -378,6 +385,7 @@
         and rows_here % HD == 0
         and (G * HD) % rows_here == 0
         and rows_here <= 8 * HD
+        and rows_here % (16 * WO_PIECES) == 0
         and key_cache.shape[1] % SCORE_BLOCK == 0
         and (hidden_in.shape[0] * (w_out.shape[1] // n // HD)) % 16 == 0
     )

time: 31.8 us -> 28.4 us (0.89)
  Pallas kernels: 28.9 us -> 26.9 us
  local copies, waits for them, and re-layouts: 2.58 us -> 1.3 us
    pallas_call x1, Pallas kernels: 28.9 us -> 26.9 us  [fused(): pl.pallas_call(functools.partial(fused_kernel, n, batch), out_shape=jax.S...]
    reshape x1 -> x0, local copies, waits for them, and re-layouts: 1.28 us -> none  [fused(): norm_gain.reshape(1, features)]
where the time goes in v2:
time: 28.4 us; the launch traced here: 28.2 us
  Pallas kernels  26.9 us (95%)
  local copies, waits for them, and re-layouts  1.3 us (5%)
    pallas_call x1, Pallas kernels, fused(): pl.pallas_call(functools.partial(fused_kernel, n, batch), out_shape=jax.S...  26.9 us
    unnamed x1, local copies, waits for them, and re-layouts  1.3 us

profile of v2, /device:TPU:0, one launch (start us, length us, event | category | flops | bytes accessed | tf_op | source)
XLA Modules:
  0.0 28.2 jit_solution(3388659912879580438)
XLA Ops:
  0.0 26.9 %shard_map.91 = bf16[4,1024]{1,0:T(4,128)(2,1)} custom-call(bf16[4,1024]{1,0:T(4,128)(2,1)} %hidden_ref.1, bf16[1024]{0:T(1024)(128)(2,1)} %gain_ref.1, s32[4]{0:T(128)} %lengths_ref.1, bf16[1024,8192]{1,0:T(8,128)(2,1)} %wq_hbm.1, bf16[1024,512]{1,0:T(8,128)(2,1)} %wk_hbm.1, bf16[1024,512]{1,0:T(8,128)(2,1)} %wv_hbm.1, bf16[512,16384]{1,0:T(8,128)(2,1)} %wo_hbm.1, ...), custom_call_target="tpu_custom_call" | custom-call | tf_op jit(solution)/shard_map/pallas_call | solution.py:341
  26.9 1.3 %copy.11 = bf16[4,1024]{1,0:T(4,128)(2,1)} copy(bf16[4,1024]{1,0:T(4,128)(2,1)} %shard_map.91) | data formatting | bytes 16384

commit v3 on v2

--- a/solution.py
+++ b/solution.py
@@ -73,9 +73,16 @@
 
 
 MSG = 24
+SPLIT = 16
+KEY_AT = 8
 QCOLS = 1024
 SCORE_BLOCK = 2048
 IN_FLIGHT = 4
+GREET_STEP = 1
+HELD = 0
+AFTER_TERMS = 2
+AFTER_CACHE = 1
+PACED = 0
 WO_PIECES = 8
 
 
@@ -152,7 +159,7 @@
     squares = jnp.broadcast_to(jnp.sum(widened * widened, axis=1, keepdims=True), (batch, HD))
     terms[...] = jnp.zeros_like(terms)
     for head in range(KVH):
-        terms[pl.ds(head * MSG + G + 2, batch, stride=KVH * MSG), :] = squares
+        terms[pl.ds(head * MSG + KEY_AT + 2, batch, stride=KVH * MSG), :] = squares
 
     key_weight_copy().wait()
     value_weight_copy().wait()
@@ -160,39 +167,47 @@
     for head in range(KVH):
         for which in range(2):
             column = which * kv_cols + head * HD
-            terms[pl.ds(head * MSG + G + which, batch, stride=KVH * MSG), :] = fresh[
+            terms[pl.ds(head * MSG + KEY_AT + which, batch, stride=KVH * MSG), :] = fresh[
                 :, column : column + HD
             ]
 
-    pl.semaphore_wait(barrier, n - 1)
-
-    def terms_copy(target):
+    def terms_copy(target, half):
         place = (me - target + n) % n - 1
+        rows = (SPLIT, MSG - SPLIT)[half]
         return pltpu.make_async_remote_copy(
-            src_ref=terms.at[pl.ds(pl.multiple_of(target * MSG, MSG), MSG)],
-            dst_ref=terms_in.at[place],
+            src_ref=terms.at[pl.ds(pl.multiple_of(target * MSG + half * SPLIT, 8), rows)],
+            dst_ref=terms_in.at[place, pl.ds(half * SPLIT, rows)],
             send_sem=a_send,
             recv_sem=a_recv,
             device_id={"wx": target},
             device_id_type=pl.DeviceIdType.MESH,
         )
 
+    ready = []
     for step in range(KVH):
         head = head_at(step)
         for half in range(halves):
             query_weight_copy(step, half).wait()
             chunk = step * halves + half
-            start_next(1)
+            if len(stream) > wo_pieces + HELD:
+                start_next(1)
             part = jnp.dot(scaled, wq[chunk], preferred_element_type=jnp.float32)
             for j in range(QCOLS // HD):
-                row = head * MSG + half * (QCOLS // HD) + j
+                row = head * MSG + half * SPLIT + j
                 terms[pl.ds(row, batch, stride=KVH * MSG), :] = part[:, j * HD : (j + 1) * HD]
-        for row in range(batch):
-            target = row * KVH + head
-
-            @pl.when(target != me)
-            def _():
-                terms_copy(target).start()
+            ready.append((head, half))
+            if step == GREET_STEP and half == 0:
+                pl.semaphore_wait(barrier, n - 1)
+            if step >= GREET_STEP:
+                for ready_head, ready_half in ready:
+                    for row in range(batch):
+                        target = row * KVH + ready_head
+
+                        @pl.when(target != me)
+                        def _():
+                            terms_copy(target, ready_half).start()
+
+                ready = []
 
     def all_terms():
         return pltpu.make_async_remote_copy(
@@ -204,19 +219,24 @@
             device_id_type=pl.DeviceIdType.MESH,
         )
 
+    start_next(HELD + AFTER_TERMS)
     for which in range(2):
         cache_copy(which).wait()
-        start_next(2)
+        start_next(AFTER_CACHE)
+    for piece in range(PACED):
+        out_weight_copy(piece).wait()
+        start_next(1)
+    all_terms().wait_recv()
     start_next(wo_pieces)
-    all_terms().wait_recv()
     total_terms = terms[pl.ds(pl.multiple_of(me * MSG, MSG), MSG), :]
     for k in range(n - 1):
         total_terms = total_terms + terms_in[k]
-    inverse = lax.rsqrt(total_terms[G + 2 : G + 3] / D + 1e-05)
-    rounded = (total_terms[: G + 2] * inverse).astype(jnp.bfloat16)
-    query = rounded[:G]
-    new_key = rounded[G : G + 1].astype(jnp.float32)
-    new_value = rounded[G + 1 : G + 2].astype(jnp.float32)
+    inverse = lax.rsqrt(total_terms[KEY_AT + 2 : KEY_AT + 3] / D + 1e-05)
+    projected = total_terms * inverse
+    query = jnp.concatenate([projected[:KEY_AT], projected[SPLIT:]], axis=0).astype(jnp.bfloat16)
+    own_terms = projected[KEY_AT:SPLIT].astype(jnp.bfloat16).astype(jnp.float32)
+    new_key = own_terms[0:1]
+    new_value = own_terms[1:2]
 
     factor = HD ** (-0.5)
     length = lengths_ref[my_row]
@@ -268,7 +288,7 @@
         def _():
             att_in[my_row] = att_out[i]
 
-    for piece in range(wo_pieces):
+    for piece in range(PACED, wo_pieces):
         out_weight_copy(piece).wait()
     for row in range(batch):
         source = row * KVH + me // sharers

time: 28.4 us -> 27.9 us (0.982)
  Pallas kernels: 26.9 us -> 26.3 us
    pallas_call x1, Pallas kernels: 26.9 us -> 26.3 us  [fused(): pl.pallas_call(functools.partial(fused_kernel, n, batch), out_shape=jax.S...]
where the time goes in v3:
time: 27.9 us; the launch traced here: 27.6 us
  Pallas kernels  26.3 us (94%)
  local copies, waits for them, and re-layouts  1.3 us (5%)
    pallas_call x1, Pallas kernels, fused(): pl.pallas_call(functools.partial(fused_kernel, n, batch), out_shape=jax.S...  26.3 us
    unnamed x1, local copies, waits for them, and re-layouts  1.3 us

profile of v3, /device:TPU:0, one launch (start us, length us, event | category | flops | bytes accessed | tf_op | source)
XLA Modules:
  0.0 27.6 jit_solution(11965706446724143880)
XLA Ops:
  0.0 26.3 %shard_map.91 = bf16[4,1024]{1,0:T(4,128)(2,1)} custom-call(bf16[4,1024]{1,0:T(4,128)(2,1)} %hidden_ref.1, bf16[1024]{0:T(1024)(128)(2,1)} %gain_ref.1, s32[4]{0:T(128)} %lengths_ref.1, bf16[1024,8192]{1,0:T(8,128)(2,1)} %wq_hbm.1, bf16[1024,512]{1,0:T(8,128)(2,1)} %wk_hbm.1, bf16[1024,512]{1,0:T(8,128)(2,1)} %wv_hbm.1, bf16[512,16384]{1,0:T(8,128)(2,1)} %wo_hbm.1, ...), custom_call_target="tpu_custom_call" | custom-call | tf_op jit(solution)/shard_map/pallas_call | solution.py:361
  26.3 1.3 %copy.11 = bf16[4,1024]{1,0:T(4,128)(2,1)} copy(bf16[4,1024]{1,0:T(4,128)(2,1)} %shard_map.91) | data formatting | bytes 16384
